TPU v7x, 512 devices: a whole 4x4x16 slice. The times are simulated.
512 devices in a mesh: dp: 2 (over core), seq: 64 (over y, z_hi, x), head: 4 (over z_lo).
Axes of the slice: x: 4, y: 4, z: 16 (z_hi: 4, z_lo: 4; z = z_hi * 4 + z_lo), core: 2. Of those that a mesh axis runs over, the one named last changes fastest.
Arguments:
- frames: bfloat16 [2, 49152, 1536], P('dp', ('seq', 'head')), may hold values from -600 to 600
- norm_gain: float32 [1536], replicated, may hold values from 0.1 to 1.9
- w_query: bfloat16 [1536, 1536], P('dp', 'head'), may hold values from -1.6 to 1.6
- w_key: bfloat16 [1536, 1536], P('dp', 'head'), may hold values from -16 to 16
- w_value: bfloat16 [1536, 1536], P('dp', 'head'), may hold values from -0.15625 to 0.15625
- w_out: bfloat16 [1536, 1536], P('head', 'dp'), may hold values from -0.4375 to 0.4375
- group_band: int32 [2, 384, 12], P('dp', 'seq'), may hold values 0 or 1
- lengths: int32 [2], P('dp'), may hold values from 24576 to 49152
Outputs:
- update: bfloat16 [2, 49152, 1536], P('dp', ('seq', 'head'))
All inputs are finite; a program needn't handle non-finite values. No bound on the sum of `group_band` on one device may be relied on, other than what follows from the above.
Results may differ from a plain program's by a relative error of at most 0.012.
Values may be sent and summed in bfloat16 or wider, within the bound.
A program may use at most 128 MiB of HBM per device.

v0:
```python
import math

import jax
import jax.numpy as jnp
from jax import lax
from jax.sharding import PartitionSpec as P

HD = 64
GROUP = 128


epsilon = 1e-05


def from_behind(value, axis, steps):
    count = lax.axis_size(axis)
    first, last = (max(0, -steps), min(count, count - steps))
    return lax.ppermute(value, axis, [(source, source + steps) for source in range(first, last)])


def layer_norm(rows, norm_gain):
    values = rows.astype(jnp.float32)
    center = values - jnp.mean(values, axis=-1, keepdims=True)
    spread = jnp.mean(center * center, axis=-1, keepdims=True)
    return (center * lax.rsqrt(spread + epsilon) * norm_gain).astype(jnp.bfloat16)


def permission(
    query_start,
    key_start,
    query_groups,
    key_groups,
    group_size,
    band_rows,
    length_value,
    total_groups,
):
    query_ids = query_start + jnp.arange(query_groups, dtype=jnp.int32)
    key_ids = key_start + jnp.arange(key_groups, dtype=jnp.int32)
    offsets = key_ids[None, :] - query_ids[:, None]
    reach_groups = band_rows.shape[1] // 2
    column = jnp.where(offsets < 0, offsets + reach_groups, offsets + reach_groups - 1)
    hits = column[:, :, None] == jnp.arange(2 * reach_groups, dtype=jnp.int32)[None, None, :]
    picked = jnp.sum(jnp.where(hits, band_rows[:, None, :], 0), axis=-1)
    inside = (key_ids >= 0) & (key_ids < total_groups)
    linked = (offsets != 0) & (jnp.abs(offsets) <= reach_groups) & inside[None, :] & (picked == 1)
    key_frames = key_start * group_size + jnp.arange(key_groups * group_size, dtype=jnp.int32)
    alive_keys = key_frames < length_value
    linked_rows = (
        jnp.repeat(jnp.repeat(linked, group_size, axis=0), group_size, axis=1) & alive_keys[None, :]
    )
    same_group = jnp.repeat(jnp.repeat(offsets == 0, group_size, axis=0), group_size, axis=1)
    return linked_rows | same_group


def local(frames, norm_gain, w_query, w_key, w_value, w_out, group_band, lengths):
    normalized = layer_norm(frames[0], norm_gain)
    gathered = lax.all_gather(normalized, "head", axis=0, tiled=True)
    rows_here = gathered.shape[0]
    local_width = w_query.shape[1]
    group_dev = group_band.shape[1]
    seq_index = lax.axis_index("seq")
    total_groups = group_dev * lax.axis_size("seq")
    query_sum = jnp.dot(
        gathered,
        lax.all_gather(w_query, "dp", axis=0, tiled=True),
        preferred_element_type=jnp.float32,
    )
    key_sum = jnp.dot(
        gathered,
        lax.all_gather(w_key, "dp", axis=0, tiled=True),
        preferred_element_type=jnp.float32,
    )
    value_sum = jnp.dot(
        gathered,
        lax.all_gather(w_value, "dp", axis=0, tiled=True),
        preferred_element_type=jnp.float32,
    )
    query_rows = query_sum.astype(jnp.bfloat16)
    own_keys = key_sum.astype(jnp.bfloat16)
    own_values = value_sum.astype(jnp.bfloat16)
    sides = []
    for distance in (1, -1):
        sides.append(from_behind((own_keys, own_values), "seq", distance))
    keys_window = jnp.concatenate([sides[0][0], own_keys, sides[1][0]], axis=0)
    values_window = jnp.concatenate([sides[0][1], own_values, sides[1][1]], axis=0)
    allowed = permission(
        seq_index * group_dev,
        seq_index * group_dev - group_dev,
        group_dev,
        3 * group_dev,
        GROUP,
        group_band[0],
        lengths[0],
        total_groups,
    )
    score_scale = 1.0 / math.sqrt(HD)

    def head_context(head_index):
        start_col = head_index * HD
        query_head = lax.dynamic_slice_in_dim(query_rows, start_col, HD, 1)
        key_head = lax.dynamic_slice_in_dim(keys_window, start_col, HD, 1)
        value_head = lax.dynamic_slice_in_dim(values_window, start_col, HD, 1)
        scores = (
            lax.dot_general(
                query_head, key_head, (((1,), (1,)), ((), ())), preferred_element_type=jnp.float32
            )
            * score_scale
        )
        masked = jnp.where(allowed, scores, -jnp.inf)
        row_max = jnp.max(masked, axis=-1, keepdims=True)
        weights = jnp.exp(masked - row_max)
        row_total = jnp.sum(weights, axis=-1, keepdims=True)
        rounded = weights.astype(jnp.bfloat16)
        return jnp.dot(rounded, value_head, preferred_element_type=jnp.float32) / row_total

    per_head = lax.map(head_context, jnp.arange(local_width // HD, dtype=jnp.int32))
    context = (
        jnp.transpose(per_head, (1, 0, 2)).reshape(rows_here, local_width).astype(jnp.bfloat16)
    )
    frame_context = lax.all_to_all(context, "head", split_axis=0, concat_axis=1, tiled=True)
    full_rows = lax.all_gather(w_out, "head", axis=0, tiled=True)
    update = jnp.dot(
        frame_context,
        lax.all_gather(full_rows, "dp", axis=1, tiled=True),
        preferred_element_type=jnp.float32,
    )
    return update.astype(jnp.bfloat16)[None]


def solution(mesh):
    return jax.shard_map(
        local,
        mesh=mesh,
        in_specs=(
            P("dp", ("seq", "head"), None),
            P(),
            P("dp", "head"),
            P("dp", "head"),
            P("dp", "head"),
            P("head", "dp"),
            P("dp", "seq", None),
            P("dp"),
        ),
        out_specs=P("dp", ("seq", "head"), None),
        check_vma=False,
    )
```

profile of v0, /device:TPU:25, one launch (start us, length us, event | category | flops | bytes accessed | tf_op | source)
XLA Modules:
  0.0 390.4 jit_solution(14620961023182381866)
XLA Ops:
  7.3 1.2 convert_reduce_fusion
  8.5 1.4 fusion.25
  9.9 1.2 fusion.27
  15.8 18.0 %all-gather.13.cloned.1.call-done = bf16[1536,384]{1,0:T(8,128)(2,1)} async-done(((bf16[768,384]{1,0:T(8,128)(2,1)}), bf16[1536,384]{1,0:T(8,128)(2,1)}) %all-gather.13.cloned.1.call-update) | async-done | bytes 1179664 | tf_op jit(solution)/shard_map/all_gather | solution.py:76
  33.8 62.4 %all-gather.7.cloned.1.call-done = bf16[768,1536]{1,0:T(8,128)(2,1)} async-done(((bf16[192,1536]{1,0:T(8,128)(2,1)}), bf16[768,1536]{1,0:T(8,128)(2,1)}) %all-gather.7.cloned.1.call-update) | async-done | bytes 2359312 | tf_op jit(solution)/shard_map/all_gather | solution.py:58
  96.3 3.4 convolution_convert_fusion.1
  99.6 3.1 collective-permute-start.2
  102.7 9.1 %collective-permute-start.3 = (bf16[768,384]{1,0:T(8,128)(2,1)S(1)}, bf16[768,384]{1,0:T(8,128)(2,1)}, u32[]{:S(2)}, u32[]{:S(2)}) collective-permute-start(bf16[768,384]{1,0:T(8,128)(2,1)S(1)} %convolution_convert_fusion.1), channel_id=1, source_target_pairs={{4,0},{8,4},{12,8},{16,12},{20,16},{24,20},{28,24},{32,28},{36,32}... | collective-permute-start | bytes 1769480 | tf_op jit(solution)/shard_map/ppermute | solution.py:18
  111.8 6.6 %all-gather.11.cloned.1.call-done = bf16[1536,384]{1,0:T(8,128)(2,1)} async-done(((bf16[768,384]{1,0:T(8,128)(2,1)}), bf16[1536,384]{1,0:T(8,128)(2,1)}) %all-gather.11.cloned.1.call-update) | async-done | bytes 1179664 | tf_op jit(solution)/shard_map/all_gather | solution.py:71
  118.4 3.4 convolution_convert_fusion.2
  121.8 3.1 collective-permute-start
  124.9 9.3 %collective-permute-start.1 = (bf16[768,384]{1,0:T(8,128)(2,1)S(1)}, bf16[768,384]{1,0:T(8,128)(2,1)}, u32[]{:S(2)}, u32[]{:S(2)}) collective-permute-start(bf16[768,384]{1,0:T(8,128)(2,1)S(1)} %convolution_convert_fusion.2), channel_id=1, source_target_pairs={{4,0},{8,4},{12,8},{16,12},{20,16},{24,20},{28,24},{32,28},{36,32}... | collective-permute-start | bytes 1769480 | tf_op jit(solution)/shard_map/ppermute | solution.py:18
  134.2 115.1 %all-gather.15.cloned.1.call-done = bf16[1536,768]{1,0:T(8,128)(2,1)} async-done(((bf16[384,768]{1,0:T(8,128)(2,1)}), bf16[1536,768]{1,0:T(8,128)(2,1)}) %all-gather.15.cloned.1.call-update) | async-done | bytes 2359312 | tf_op jit(solution)/shard_map/all_gather | solution.py:122
  249.4 19.4 %all-gather.9.cloned.1.call-done = bf16[1536,384]{1,0:T(8,128)(2,1)} async-done(((bf16[768,384]{1,0:T(8,128)(2,1)}), bf16[1536,384]{1,0:T(8,128)(2,1)}) %all-gather.9.cloned.1.call-update) | async-done | bytes 1179664 | tf_op jit(solution)/shard_map/all_gather | solution.py:66
  268.8 4.2 %convolution_convert_fusion.3 = bf16[768,384]{1,0:T(8,128)(2,1)} fusion(bf16[768,1536]{1,0:T(8,128)(2,1)} %all-gather.7.cloned.1.call-done, bf16[1536,384]{1,0:T(8,128)(2,1)} %all-gather.9.cloned.1.call-done), kind=kOutput, calls=%fused_computation.23 | convolution fusion | flops 906264576 | bytes 4128768 | tf_op jit(solution)/shard_map/dot_general | solution.py:64
  273.0 1.3 pad_maximum_fusion.1
  274.4 1.4 pad_maximum_fusion
  275.8 80.6 %while.11 = (s32[]{:T(128)}, bf16[6,768,64]{1,2,0:T(8,128)(2,1)}, s32[6]{0:T(128)S(1)}, bf16[768,384]{1,0:T(8,128)(2,1)}, bf16[2304,384]{1,0:T(8,128)(2,1)S(1)},...) while((s32[]{:T(128)}, bf16[6,768,64]{1,2,0:T(8,128)(2,1)}, ...), condition=%wide.region_6.7_spmd.clone, body=%wide.region_3.6_spmd.clone.sunk | while | flops 468957696 | bytes 37067480 | solution.py:117
  278.6 1.9 copy.32
  281.0 1.9 copy.33
  282.9 3.3 fusion.49
  287.2 2.2 fusion.51
  290.8 1.2 broadcast_in_dim.77
  292.0 1.9 copy.32
  294.4 1.9 copy.33
  296.3 3.3 fusion.49
  300.7 2.2 fusion.51
  305.4 1.9 copy.32
  307.8 1.9 copy.33
  309.7 3.3 fusion.49
  314.1 2.2 fusion.51
  317.6 1.2 broadcast_in_dim.77
  318.8 1.9 copy.32
  321.2 1.9 copy.33
  323.1 3.3 fusion.49
  327.5 2.2 fusion.51
  331.0 1.2 broadcast_in_dim.77
  332.2 1.9 copy.32
  334.6 1.9 copy.33
  336.5 3.3 fusion.49
  340.9 2.2 fusion.51
  345.6 1.9 copy.32
  348.0 1.9 copy.33
  349.9 3.3 fusion.49
  354.3 2.2 fusion.51
  356.4 2.3 convert_element_type.42
  359.6 19.6 %all_to_all.16 = bf16[4,192,384]{2,1,0:T(8,128)(2,1)S(1)} all-to-all(bf16[4,192,384]{2,1,0:T(8,128)(2,1)S(1)} %copy.22), channel_id=1, replica_groups=mesh['dp'=2,'seq'=64,'head'=4] {'head'}, dimensions={0} | all-to-all | bytes 1179648 | tf_op jit(solution)/shard_map/all_to_all | solution.py:121
  379.3 4.2 %fusion.21 = bf16[1,192,1536]{2,1,0:T(8,128)(2,1)} fusion(bf16[192,1536]{1,0:T(8,128)(2,1)S(1)} %bitcast.69, bf16[1536,1536]{1,0:T(8,128)(2,1)} %all-gather.17.cloned.1.call-done), kind=kOutput, calls=%fused_computation.16 | convolution fusion | flops 906264576 | bytes 5898240 | tf_op jit(solution)/shard_map/dot_general | solution.py:123
  (82 shorter events, 22.6 us)
Async XLA Ops:
  6.5 3.4 copy-start
  6.5 3.4 copy-start.4
  6.5 27.3 %all-gather.13.cloned.1.call-start = ((), (), s32[]{:S(2)}) async-start(), calls=%async_computation.4 | async-start | bytes 1769472 | tf_op jit(solution)/shard_map/all_gather | solution.py:76
  7.3 89.0 %all-gather.7.cloned.1.call-start = ((), (), s32[]{:S(2)}) async-start(), calls=%async_computation.1 | async-start | bytes 2949120 | tf_op jit(solution)/shard_map/all_gather | solution.py:58
  9.9 3.3 copy-start.5
  11.2 107.2 %all-gather.11.cloned.1.call-start = ((), (), s32[]{:S(2)}) async-start(), calls=%async_computation.3 | async-start | bytes 1769472 | tf_op jit(solution)/shard_map/all_gather | solution.py:71
  11.9 237.4 %all-gather.15.cloned.1.call-start = ((), (), s32[]{:S(2)}) async-start(), calls=%async_computation.5 | async-start | bytes 2949120 | tf_op jit(solution)/shard_map/all_gather | solution.py:122
  12.5 256.3 %all-gather.9.cloned.1.call-start = ((), (), s32[]{:S(2)}) async-start(), calls=%async_computation.2 | async-start | bytes 1769472 | tf_op jit(solution)/shard_map/all_gather | solution.py:66
  13.1 366.2 %all-gather.17.cloned.1.call-start = ((), (), s32[]{:S(2)}) async-start(), calls=%async_computation.6 | async-start | bytes 7077888 | tf_op jit(solution)/shard_map/all_gather | solution.py:125
  99.6 173.4 %collective-permute-start.2 = (bf16[768,384]{1,0:T(8,128)(2,1)S(1)}, bf16[768,384]{1,0:T(8,128)(2,1)S(1)}, u32[]{:S(2)}, u32[]{:S(2)}) collective-permute-start(bf16[768,384]{1,0:T(8,128)(2,1)S(1)} %convolution_convert_fusion.1), channel_id=1, source_target_pairs={{0,4},{4,8},{8,12},{12,16},{16,20},{20,24},{24,28},{28,32},{32,36}... | collective-permute-start | bytes 1769480 | tf_op jit(solution)/shard_map/ppermute | solution.py:18
  102.7 170.3 %collective-permute-start.3 = (bf16[768,384]{1,0:T(8,128)(2,1)S(1)}, bf16[768,384]{1,0:T(8,128)(2,1)}, u32[]{:S(2)}, u32[]{:S(2)}) collective-permute-start(bf16[768,384]{1,0:T(8,128)(2,1)S(1)} %convolution_convert_fusion.1), channel_id=1, source_target_pairs={{4,0},{8,4},{12,8},{16,12},{20,16},{24,20},{28,24},{32,28},{36,32}... | collective-permute-start | bytes 1769480 | tf_op jit(solution)/shard_map/ppermute | solution.py:18
  121.8 151.2 %copy-start.2 = (bf16[768,384]{1,0:T(8,128)(2,1)}, bf16[768,384]{1,0:T(8,128)(2,1)S(1)}, u32[]{:S(2)}) copy-start(bf16[768,384]{1,0:T(8,128)(2,1)S(1)} %convolution_convert_fusion.2) | copy-start | bytes 1769476
  121.8 152.5 %collective-permute-start = (bf16[768,384]{1,0:T(8,128)(2,1)S(1)}, bf16[768,384]{1,0:T(8,128)(2,1)}, u32[]{:S(2)}, u32[]{:S(2)}) collective-permute-start(bf16[768,384]{1,0:T(8,128)(2,1)S(1)} %convolution_convert_fusion.2), channel_id=1, source_target_pairs={{0,4},{4,8},{8,12},{12,16},{16,20},{20,24},{24,28},{28,32},{32,36}... | collective-permute-start | bytes 1769480 | tf_op jit(solution)/shard_map/ppermute | solution.py:18
  124.9 149.5 %collective-permute-start.1 = (bf16[768,384]{1,0:T(8,128)(2,1)S(1)}, bf16[768,384]{1,0:T(8,128)(2,1)}, u32[]{:S(2)}, u32[]{:S(2)}) collective-permute-start(bf16[768,384]{1,0:T(8,128)(2,1)S(1)} %convolution_convert_fusion.2), channel_id=1, source_target_pairs={{4,0},{8,4},{12,8},{16,12},{20,16},{24,20},{28,24},{32,28},{36,32}... | collective-permute-start | bytes 1769480 | tf_op jit(solution)/shard_map/ppermute | solution.py:18
  273.0 1.3 copy-start.3
  278.5 1.9 copy-start.1
  292.0 1.9 copy-start.1
  305.4 1.9 copy-start.1
  318.8 1.9 copy-start.1
  332.2 1.9 copy-start.1
  345.6 1.9 copy-start.1
Sparse Core Ops, SparseCore 0:
  9.4 24.3 all-gather.12
  35.9 60.2 all-gather.6
  98.3 20.0 all-gather.10
  120.4 128.9 all-gather.14
  251.3 17.4 all-gather.8
  270.8 26.2 all-gather.16
where the time goes:
time: 393 us; the launch traced here: 390 us
  waiting for transfers between devices  224 us (57%)
  matrix products  47.7 us (12%)
  local copies, waits for them, and re-layouts  41.7 us (11%)
  starting transfers between devices  24.8 us (6%)
  blocking collectives  19.6 us (5%)
  between operations  14.4 us (4%)
  other arithmetic  13.4 us (3%)
  loops' own time  4.66 us (1%)
    all_gather x1, waiting for transfers between devices, local(): full_rows = lax.all_gather(w_out, 'head', axis=0, tiled=True)  115 us
    all_gather x1, waiting for transfers between devices, local(): gathered = lax.all_gather(normalized, 'head', axis=0, tiled=True)  62.4 us
    ppermute x4, starting transfers between devices, from_behind(): lax.ppermute(value, axis, [(source, source + steps) for source in range(f...  24.6 us
    dot_general x6, matrix products, head_context(): lax.dot_general(query_head, key_head, (((1,), (1,)), ((), ())), preferred...  19.7 us
    all_to_all x1, blocking collectives, local(): lax.all_to_all(context, 'head', split_axis=0, concat_axis=1, tiled=True)  19.6 us
    all_gather x1, waiting for transfers between devices, local(): lax.all_gather(w_query, 'dp', axis=0, tiled=True)  19.4 us
    all_gather x1, waiting for transfers between devices, local(): lax.all_gather(w_value, 'dp', axis=0, tiled=True)  18 us
    dot_general x6, matrix products, head_context(): jnp.dot(rounded, value_head, preferred_element_type=jnp.float32) / row_total  12.9 us
  transfers between devices with their start and end apart: 10, of which 5 were waited for; matrix products, arithmetic and copies ran while one was open for 25% of the time, Pallas kernels for 0%

commit v1 on v0

v1 whole, which is shorter than its diff:
```python
import functools

import jax
import jax.numpy as jnp
from jax import lax
from jax.experimental import pallas as pl
from jax.experimental.pallas import tpu as pltpu
from jax.sharding import PartitionSpec as P

MESH = pl.DeviceIdType.MESH
HD = 64
GROUP = 128
ROWS = 192
RUN = 768
WIDTH = 384
D = 1536
REACH = 6
PIECE = 48
QB = 256
FORBIDDEN = -1e30
epsilon = 1e-05


def kernel(
    frames, gain, w_query, w_key, w_value, band, lengths, out,
    weights, normalized, query, kv, bias, onehot, acc, top, context, gathered, relay_up, relay_down,
    w_send, w_recv, w_local, left_send, right_send, block_recv,
    up_send, up_recv, down_send, down_recv,
    spread_up_send, spread_up_recv, spread_down_send, spread_down_recv,
    far_up_send, far_up_recv, far_down_send, far_down_recv,
    ctx_send, ctx_recv,
):
    dp, seq, head = lax.axis_index("dp"), lax.axis_index("seq"), lax.axis_index("head")
    row, x = seq // 4, seq % 4
    first_seq = row * 4
    has_up, has_down = row < 15, row > 0

    def copy(src, dst, send, recv, to):
        return pltpu.make_async_remote_copy(
            src_ref=src, dst_ref=dst, send_sem=send, recv_sem=recv, device_id=to, device_id_type=MESH
        )

    barrier = pltpu.get_barrier_semaphore()

    def greet(to):
        pl.semaphore_signal(barrier, inc=1, device_id=to, device_id_type=MESH)

    greet((1 - dp, seq, head))
    for k in (1, 2, 3):
        greet((dp, seq, (head + k) % 4))
        greet((dp, first_seq + (x + k) % 4, head))

    @pl.when((x == 0) & has_down)
    def _():
        for q in range(4):
            greet((dp, first_seq - 4 + q, head))

    @pl.when((x == 3) & has_up)
    def _():
        for q in range(4):
            greet((dp, first_seq + 4 + q, head))

    pl.semaphore_wait(barrier, 7 + (1 - (row + 1) // 16) + (row + 15) // 16)

    half = pl.ds(pl.multiple_of(dp * (D // 2), D // 2), D // 2)

    def weight_there(i, ref):
        part = weights.at[half, pl.ds(i * WIDTH, WIDTH)]
        return copy(ref, part, w_send.at[i], w_recv.at[i], (1 - dp, seq, head))

    def weight_here(i, ref):
        return pltpu.make_async_copy(ref, weights.at[half, pl.ds(i * WIDTH, WIDTH)], w_local.at[i])

    for i, ref in enumerate((w_query, w_key, w_value)):
        weight_there(i, ref).start()
        weight_here(i, ref).start()

    values = frames[...].astype(jnp.float32)
    center = values - jnp.mean(values, axis=-1, keepdims=True)
    spread = jnp.mean(center * center, axis=-1, keepdims=True)
    normalized[head] = (center * lax.rsqrt(spread + epsilon) * gain[...]).astype(jnp.bfloat16)

    has_left, has_right = head > 0, head < 3
    left = (dp, seq, (head + 3) % 4)
    right = (dp, seq, (head + 1) % 4)

    def to_left(b):
        return copy(normalized.at[b], normalized.at[b], left_send.at[b], block_recv.at[b], left)

    def to_right(b):
        return copy(normalized.at[b], normalized.at[b], right_send.at[b], block_recv.at[b], right)

    pl.when(has_left)(lambda: to_left(head).start())
    pl.when(has_right)(lambda: to_right(head).start())

    onehot[...] = (
        lax.broadcasted_iota(jnp.int32, (RUN, 128), 0) // GROUP
        == lax.broadcasted_iota(jnp.int32, (RUN, 128), 1)
    ).astype(jnp.bfloat16)
    lane = lax.broadcasted_iota(jnp.int32, (1, 128), 1)
    within = lax.broadcasted_iota(jnp.int32, (GROUP, 128), 0)
    for kg in range(3 * REACH):
        seen = jnp.zeros((1, 128), jnp.int32)
        own = jnp.zeros((1, 128), jnp.int32)
        for g in range(REACH):
            offset = kg - REACH - g
            if offset == 0:
                own = jnp.where(lane == g, 1, own)
            elif abs(offset) <= REACH:
                column = offset + REACH if offset < 0 else offset + REACH - 1
                seen = jnp.where(lane == g, band[g, column], seen)
        group = seq * REACH - REACH + kg
        inside = jnp.where((group >= 0) & (group < 64 * REACH), 1, 0)
        alive = (group * GROUP + within < lengths[0]).astype(jnp.int32) * inside
        allowed = (jnp.where(seen == 1, 1, 0) * alive + own) > 0
        bias[kg * GROUP:(kg + 1) * GROUP, :] = jnp.where(allowed, 0.0, FORBIDDEN).astype(jnp.bfloat16)

    @pl.when(seq == 0)
    def _():
        kv[0:RUN, :] = jnp.zeros((RUN, 2 * WIDTH), jnp.bfloat16)

    @pl.when(seq == 63)
    def _():
        kv[2 * RUN:3 * RUN, :] = jnp.zeros((RUN, 2 * WIDTH), jnp.bfloat16)

    for i, ref in enumerate((w_query, w_key, w_value)):
        weight_here(i, ref).wait()
        weight_there(i, ref).wait_recv()

    def place(side, b, q=None):
        start, size = side * RUN + b * ROWS, ROWS
        if q is not None:
            start, size = start + q * PIECE, PIECE
        return kv.at[pl.ds(pl.multiple_of(start, 16), size), :]

    def up_near(b):
        return copy(place(1, b), place(0, b), up_send.at[b], up_recv.at[b], (dp, (seq + 1) % 64, head))

    def down_near(b):
        return copy(place(1, b), place(2, b), down_send.at[b], down_recv.at[b], (dp, (seq + 63) % 64, head))

    def up_spread(b, q):
        return copy(
            place(1, b, q), relay_up.at[b], spread_up_send.at[b, q], spread_up_recv.at[b], (dp, first_seq + q, head)
        )

    def down_spread(b, q):
        return copy(
            place(1, b, q), relay_down.at[b], spread_down_send.at[b, q], spread_down_recv.at[b],
            (dp, first_seq + q, head),
        )

    def up_far(b, src, q):
        return copy(src, place(0, b, q), far_up_send.at[b], far_up_recv.at[b, q], (dp, (first_seq + 4) % 64, head))

    def down_far(b, src, q):
        return copy(src, place(2, b, q), far_down_send.at[b], far_down_recv.at[b, q], (dp, (first_seq + 63) % 64, head))

    sends_up_far, sends_down_far = (x == 3) & has_up, (x == 0) & has_down
    relays_up, relays_down = (x < 3) & has_up, (x > 0) & has_down

    def send_block(b):
        pl.when(x < 3)(lambda: up_near(b).start())
        pl.when(x > 0)(lambda: down_near(b).start())

        @pl.when(sends_up_far)
        def _():
            for q in range(3):
                up_spread(b, q).start()
            up_far(b, place(1, b, 3), 3).start()

        @pl.when(sends_down_far)
        def _():
            for q in range(1, 4):
                down_spread(b, q).start()
            down_far(b, place(1, b, 0), 0).start()

    def relay_block(b):
        @pl.when(relays_up)
        def _():
            up_spread(b, x).wait_recv()
            up_far(b, relay_up.at[b], x).start()

        @pl.when(relays_down)
        def _():
            down_spread(b, x).wait_recv()
            down_far(b, relay_down.at[b], x).start()

    far_end = head // 2
    mirrored = head + far_end * (3 - 2 * head)

    def nth(t):
        near = t // 2 * 2 + (t + mirrored * (1 - t // 2)) % 2
        return near + far_end * (3 - 2 * near)

    def project(t, carry):
        b = nth(t)

        @pl.when(t > 0)
        def _():
            to_left(b).wait_recv()
            pl.when((b < head) & has_right)(lambda: to_right(b).start())
            pl.when((b > head) & has_left)(lambda: to_left(b).start())

        rows = normalized[b]
        product = jnp.dot(rows, weights[...], preferred_element_type=jnp.float32).astype(jnp.bfloat16)
        start = pl.multiple_of(b * ROWS, ROWS)
        query[pl.ds(start, ROWS), :] = product[:, :WIDTH] * jnp.bfloat16(0.125)
        kv[pl.ds(pl.multiple_of(RUN + start, ROWS), ROWS), :] = product[:, WIDTH:]
        send_block(b)
        pl.when(t > 0)(lambda: relay_block(nth((t + 3) % 4)))
        return carry

    lax.fori_loop(0, 4, project, 0)

    low_half = lax.broadcasted_iota(jnp.int32, (QB, 128), 1) < HD

    def attend(p, query_start, key_start, keys, first):
        lanes = pl.ds(pl.multiple_of(p * 128, 128), 128)
        value_lanes = pl.ds(pl.multiple_of(WIDTH + p * 128, 128), 128)
        key_rows = pl.ds(pl.multiple_of(key_start, QB), keys)
        query_rows = pl.ds(pl.multiple_of(query_start, QB), QB)
        key_tile = jnp.concatenate([kv[key_rows, lanes], bias[key_rows, :]], axis=1)
        value_tile = jnp.concatenate([kv[key_rows, value_lanes], jnp.ones((keys, 128), jnp.bfloat16)], axis=1)
        query_tile = query[query_rows, lanes]
        marks = onehot[query_rows, :]
        for hh in range(2):
            h = p * 2 + hh
            mine = jnp.where(low_half == (hh == 0), query_tile, jnp.zeros_like(query_tile))
            scores = lax.dot_general(
                jnp.concatenate([mine, marks], axis=1), key_tile, (((1,), (1,)), ((), ())),
                preferred_element_type=jnp.float32,
            )
            here = jnp.max(scores, axis=-1, keepdims=True)
            if first:
                best = here
            else:
                before = top[h, query_rows, :][:, :1]
                best = jnp.maximum(before, here)
            rounded = jnp.exp(scores - best).astype(jnp.bfloat16)
            part = jnp.dot(rounded, value_tile, preferred_element_type=jnp.float32)
            if not first:
                part = part + acc[h, query_rows, :] * jnp.exp(before - best)
            acc[h, query_rows, :] = part
            top[h, query_rows, :] = jnp.broadcast_to(best, (QB, 128))

    def own_part(p, carry):
        for j in range(3):
            attend(p, j * QB, RUN, RUN, True)
        pl.when(p == 0)(lambda: relay_block(nth(3)))
        return carry

    lax.fori_loop(0, 3, own_part, 0)

    def wait_side(side):
        @pl.when(side == 0)
        def _():
            @pl.when(x > 0)
            def _():
                for b in range(4):
                    up_near(b).wait_recv()

            @pl.when((x == 0) & has_down)
            def _():
                for b in range(4):
                    for q in range(4):
                        up_far(b, place(1, b, q), q).wait_recv()

        @pl.when(side == 1)
        def _():
            @pl.when(x < 3)
            def _():
                for b in range(4):
                    down_near(b).wait_recv()

            @pl.when((x == 3) & has_up)
            def _():
                for b in range(4):
                    for q in range(4):
                        down_far(b, place(1, b, q), q).wait_recv()

    def side_part(p, side):
        for j in range(3):
            query_start = j * QB + side * (2 * QB - 2 * j * QB)
            key_start = j * QB + side * (2 * RUN - j * QB)
            attend(p, query_start, key_start, RUN - j * QB, False)

    first_side = 1 - (x + 3) // 4
    wait_side(first_side)

    def early_part(p, carry):
        side_part(p, first_side)
        return carry

    lax.fori_loop(0, 3, early_part, 0)
    last_side = 1 - first_side
    wait_side(last_side)

    def ctx_copy(p, k):
        to = (head + k) % 4
        return copy(
            context.at[pl.ds(pl.multiple_of(to * ROWS, ROWS), ROWS), pl.ds(pl.multiple_of(p * 128, 128), 128)],
            gathered.at[:, pl.ds(pl.multiple_of(head * WIDTH + p * 128, 128), 128)],
            ctx_send.at[p, k - 1], ctx_recv.at[p, k - 1], (dp, seq, to),
        )

    def late_part(p, carry):
        side_part(p, last_side)
        lanes = pl.ds(pl.multiple_of(p * 128, 128), 128)
        for j in range(3):
            rows = pl.ds(j * QB, QB)
            low, high = acc[p * 2, rows, :], acc[p * 2 + 1, rows, :]
            context[rows, lanes] = jnp.where(
                low_half, low[:, :128] / low[:, 128:], high[:, :128] / high[:, 128:]
            ).astype(jnp.bfloat16)
        for k in (2, 1, 3):
            ctx_copy(p, k).start()
        return carry

    lax.fori_loop(0, 3, late_part, 0)
    own_lanes = pl.ds(pl.multiple_of(head * WIDTH, 128), WIDTH)
    gathered[:, own_lanes] = context[pl.ds(pl.multiple_of(head * ROWS, ROWS), ROWS), :]

    for i, ref in enumerate((w_query, w_key, w_value)):
        weight_there(i, ref).wait_send()
    for b in range(4):
        pl.when((b <= head) & has_right)(lambda: to_right(b).wait_send())
        pl.when((b >= head) & has_left)(lambda: to_left(b).wait_send())
        pl.when(x < 3)(lambda: up_near(b).wait_send())
        pl.when(x > 0)(lambda: down_near(b).wait_send())

        @pl.when(sends_up_far)
        def _():
            for q in range(3):
                up_spread(b, q).wait_send()

        @pl.when(sends_down_far)
        def _():
            for q in range(1, 4):
                down_spread(b, q).wait_send()

        pl.when(has_up)(lambda: up_far(b, place(1, b, 3), 3).wait_send())
        pl.when(has_down)(lambda: down_far(b, place(1, b, 0), 0).wait_send())
    for p in range(3):
        for k in (1, 2, 3):
            ctx_copy(p, k).wait()
    out[...] = gathered[...]


def exchange_and_attend(frames, gain, w_query, w_key, w_value, band, lengths):
    vmem, smem, anywhere = (pl.BlockSpec(memory_space=m) for m in (pltpu.VMEM, pltpu.SMEM, pl.ANY))
    dma = pltpu.SemaphoreType.DMA
    bf16, f32 = jnp.bfloat16, jnp.float32
    return pl.pallas_call(
        kernel,
        out_shape=jax.ShapeDtypeStruct((ROWS, D), bf16),
        in_specs=[vmem, vmem, anywhere, anywhere, anywhere, smem, smem],
        out_specs=vmem,
        scratch_shapes=[
            pltpu.VMEM((D, 3 * WIDTH), bf16),
            pltpu.VMEM((4, ROWS, D), bf16),
            pltpu.VMEM((RUN, WIDTH), bf16),
            pltpu.VMEM((3 * RUN, 2 * WIDTH), bf16),
            pltpu.VMEM((3 * RUN, 128), bf16),
            pltpu.VMEM((RUN, 128), bf16),
            pltpu.VMEM((6, RUN, 256), f32),
            pltpu.VMEM((6, RUN, 128), f32),
            pltpu.VMEM((RUN, WIDTH), bf16),
            pltpu.VMEM((ROWS, D), bf16),
            pltpu.VMEM((4, PIECE, 2 * WIDTH), bf16),
            pltpu.VMEM((4, PIECE, 2 * WIDTH), bf16),
            dma((3,)), dma((3,)), dma((3,)),
            dma((4,)), dma((4,)), dma((4,)),
            dma((4,)), dma((4,)), dma((4,)), dma((4,)),
            dma((4, 4)), dma((4,)), dma((4, 4)), dma((4,)),
            dma((4,)), dma((4, 4)), dma((4,)), dma((4, 4)),
            dma((3, 3)), dma((3, 3)),
        ],
        compiler_params=pltpu.CompilerParams(
            collective_id=0, has_side_effects=True, vmem_limit_bytes=48 * 2**20
        ),
        cost_estimate=pl.CostEstimate(flops=60_000_000_000, bytes_accessed=8_000_000, transcendentals=8_000_000),
        name="attend",
    )(frames, gain, w_query, w_key, w_value, band, lengths)


def local(frames, norm_gain, w_query, w_key, w_value, w_out, group_band, lengths):
    frame_context = exchange_and_attend(
        frames[0], norm_gain[None], w_query, w_key, w_value, group_band[0], lengths
    )
    full_rows = lax.all_gather(w_out, "head", axis=0, tiled=True)
    update = jnp.dot(
        frame_context,
        lax.all_gather(full_rows, "dp", axis=1, tiled=True),
        preferred_element_type=jnp.float32,
    )
    return update.astype(jnp.bfloat16)[None]


def solution(mesh):
    return jax.shard_map(
        local,
        mesh=mesh,
        in_specs=(
            P("dp", ("seq", "head"), None),
            P(),
            P("dp", "head"),
            P("dp", "head"),
            P("dp", "head"),
            P("head", "dp"),
            P("dp", "seq", None),
            P("dp"),
        ),
        out_specs=P("dp", ("seq", "head"), None),
        check_vma=False,
    )
```

time: 393 us -> 198 us (0.50)
  the two profiles are of different devices: /device:TPU:25 before, /device:TPU:396 now
where the time goes in v1:
time: 198 us
  Pallas kernels  115 us (58%)
  waiting for transfers between devices  58.6 us (30%)
  between operations  14.1 us (7%)
  local copies, waits for them, and re-layouts  5.64 us (3%)
  matrix products  4.26 us (2%)
    pallas_call x1, Pallas kernels, exchange_and_attend(): pl.pallas_call(kernel, out_shape=jax.ShapeDtypeStruct((ROWS, D), bf16), i...  115 us
    all_gather x1, waiting for transfers between devices, local(): full_rows = lax.all_gather(w_out, 'head', axis=0, tiled=True)  57.9 us
    unnamed x9, local copies, waits for them, and re-layouts  4.94 us
    dot_general x1, matrix products, local(): jnp.dot(frame_context, lax.all_gather(full_rows, 'dp', axis=1, tiled=True...  4.26 us
  transfers between devices with their start and end apart: 2, of which 1 were waited for; matrix products, arithmetic and copies ran while one was open for 1% of the time, Pallas kernels for 58%

profile of v1, /device:TPU:396, one launch (start us, length us, event | category | flops | bytes accessed | tf_op | source)
XLA Modules:
  0.0 197.7 jit_solution(5861266424554566832)
XLA Ops:
  6.5 0.0 all-gather.3.cloned.1.call-start
  6.5 0.7 all-gather.3.cloned.1.call-update
  7.3 0.0 all-gather.5.cloned.1.call-start
  7.9 0.7 copy.11
  8.6 0.7 broadcast_in_dim.6.gain
  9.3 57.9 %all-gather.3.cloned.1.call-done = bf16[1536,768]{1,0:T(8,128)(2,1)} async-done(((bf16[384,768]{1,0:T(8,128)(2,1)}), bf16[1536,768]{1,0:T(8,128)(2,1)}) %all-gather.3.cloned.1.call-update) | async-done | bytes 2359312 | tf_op jit(solution)/shard_map/all_gather | solution.py:391
  67.2 0.0 all-gather.5.cloned.1.call-update
  67.2 0.0 copy-start
  67.3 1.1 copy-done
  68.3 0.0 copy-start.1
  68.3 1.1 copy-done.1
  69.4 0.0 copy-start.2
  69.4 1.1 copy-done.2
  70.4 0.0 copy-start.3
  70.4 1.1 copy-done.3
  71.5 115.1 %attend.1 = bf16[192,1536]{1,0:T(8,128)(2,1)S(1)} custom-call(bf16[192,1536]{1,0:T(8,128)(2,1)S(1)} %bitcast.9, f32[1,1536]{1,0:T(1,128)S(1)} %broadcast_in_dim.6.gain, bf16[768,384]{1,0:T(8,128)(2,1)S(1)} %copy-done.1, bf16[768,384]{1,0:T(8,128)(2,1)S(1)} %copy-done.2, bf16[768,384]{1,0:T(8,128)(2,1)S(1)} %copy-done.3, s32[6,12]{1,0:T(8,128)S(1)} %bitcast.8, ...), custom_call_target="tpu_custom_call" | custom-call | flops 60000002048 | bytes 8000000 | tf_op jit(solution)/shard_map/attend/pallas_call | solution.py:354
  186.6 0.0 all-gather.5.cloned.1.call-done
  186.6 4.3 %fusion = bf16[1,192,1536]{2,1,0:T(8,128)(2,1)} fusion(bf16[192,1536]{1,0:T(8,128)(2,1)S(1)} %attend.1, bf16[1536,1536]{1,0:T(8,128)(2,1)} %all-gather.5.cloned.1.call-done), kind=kOutput, calls=%fused_computation.1 | convolution fusion | flops 906264576 | bytes 5898240 | tf_op jit(solution)/shard_map/dot_general | solution.py:392
Async XLA Ops:
  6.5 60.7 %all-gather.3.cloned.1.call-start = ((), (), s32[]{:S(2)}) async-start(), calls=%async_computation | async-start | bytes 2949120 | tf_op jit(solution)/shard_map/all_gather | solution.py:391
  7.3 179.4 %all-gather.5.cloned.1.call-start = ((), (), s32[]{:S(2)}) async-start(), calls=%async_computation.1 | async-start | bytes 7077888 | tf_op jit(solution)/shard_map/all_gather | solution.py:394
  67.2 1.1 copy-start
  68.3 1.1 copy-start.1
  69.4 1.1 copy-start.2
  70.4 1.1 copy-start.3
Sparse Core Ops, SparseCore 0:
  9.5 57.7 all-gather.2
  69.3 26.4 all-gather.4

commit v2 on v1

--- a/solution.py
+++ b/solution.py
@@ -22,16 +22,18 @@
 
 
 def kernel(
-    frames, gain, w_query, w_key, w_value, band, lengths, out,
-    weights, normalized, query, kv, bias, onehot, acc, top, context, gathered, relay_up, relay_down,
+    frames, gain, w_query, w_key, w_value, w_out, band, lengths, out,
+    weights, normalized, query, kv, bias, onehot, acc, top, context, gathered, relay_up, relay_down, projection,
     w_send, w_recv, w_local, left_send, right_send, block_recv,
     up_send, up_recv, down_send, down_recv,
     spread_up_send, spread_up_recv, spread_down_send, spread_down_recv,
     far_up_send, far_up_recv, far_down_send, far_down_recv,
     ctx_send, ctx_recv,
+    out_local, out_z_send, out_z_recv, out_x_send, out_x_recv, out_y_send, out_y_recv, out_core_send, out_core_recv,
 ):
     dp, seq, head = lax.axis_index("dp"), lax.axis_index("seq"), lax.axis_index("head")
     row, x = seq // 4, seq % 4
+    y = seq // 16
     first_seq = row * 4
     has_up, has_down = row < 15, row > 0
 
@@ -49,6 +51,7 @@
     for k in (1, 2, 3):
         greet((dp, seq, (head + k) % 4))
         greet((dp, first_seq + (x + k) % 4, head))
+        greet((dp, (seq + 16 * k) % 64, head))
 
     @pl.when((x == 0) & has_down)
     def _():
@@ -60,7 +63,7 @@
         for q in range(4):
             greet((dp, first_seq + 4 + q, head))
 
-    pl.semaphore_wait(barrier, 7 + (1 - (row + 1) // 16) + (row + 15) // 16)
+    pl.semaphore_wait(barrier, 10 + (1 - (row + 1) // 16) + (row + 15) // 16)
 
     half = pl.ds(pl.multiple_of(dp * (D // 2), D // 2), D // 2)
 
@@ -74,6 +77,38 @@
     for i, ref in enumerate((w_query, w_key, w_value)):
         weight_there(i, ref).start()
         weight_here(i, ref).start()
+
+    piece_rows = pl.ds(pl.multiple_of(y * 96 + x % 2 * 48, 16), 48)
+    strip_rows = pl.ds(pl.multiple_of(y * 96, 16), 96)
+    piece_from = pl.ds(pl.multiple_of(x // 2 * WIDTH, 128), WIDTH)
+    piece_columns = pl.ds(pl.multiple_of(dp * (D // 2) + x // 2 * WIDTH, 128), WIDTH)
+
+    def out_here():
+        return pltpu.make_async_copy(
+            w_out.at[piece_rows, piece_from], projection.at[head, piece_rows, piece_columns], out_local
+        )
+
+    def out_z(k):
+        return copy(
+            w_out.at[piece_rows, piece_from], projection.at[head, piece_rows, piece_columns],
+            out_z_send.at[k - 1], out_z_recv.at[k - 1], (dp, seq, (head + k) % 4),
+        )
+
+    def out_x(k):
+        part = projection.at[:, piece_rows, piece_columns]
+        return copy(part, part, out_x_send.at[k - 1], out_x_recv.at[k - 1], (dp, first_seq + (x + k) % 4, head))
+
+    def out_y(k):
+        part = projection.at[:, strip_rows, half]
+        return copy(part, part, out_y_send.at[k - 1], out_y_recv.at[k - 1], (dp, (seq + 16 * k) % 64, head))
+
+    def out_core():
+        part = projection.at[:, :, half]
+        return copy(part, part, out_core_send, out_core_recv, (1 - dp, seq, head))
+
+    out_here().start()
+    for k in (2, 1, 3):
+        out_z(k).start()
 
     values = frames[...].astype(jnp.float32)
     center = values - jnp.mean(values, axis=-1, keepdims=True)
@@ -201,6 +236,21 @@
             to_left(b).wait_recv()
             pl.when((b < head) & has_right)(lambda: to_right(b).start())
             pl.when((b > head) & has_left)(lambda: to_left(b).start())
+
+        @pl.when(t == 1)
+        def _():
+            out_here().wait()
+            for k in (1, 2, 3):
+                out_z(k).wait_recv()
+            for k in (2, 1, 3):
+                out_x(k).start()
+
+        @pl.when(t == 2 + mirrored)
+        def _():
+            for k in (1, 2, 3):
+                out_x(k).wait_recv()
+            for k in (2, 1, 3):
+                out_y(k).start()
 
         rows = normalized[b]
         product = jnp.dot(rows, weights[...], preferred_element_type=jnp.float32).astype(jnp.bfloat16)
@@ -293,6 +343,9 @@
         return carry
 
     lax.fori_loop(0, 3, early_part, 0)
+    for k in (1, 2, 3):
+        out_y(k).wait_recv()
+    out_core().start()
     last_side = 1 - first_side
     wait_side(last_side)
 
@@ -341,20 +394,30 @@
 
         pl.when(has_up)(lambda: up_far(b, place(1, b, 3), 3).wait_send())
         pl.when(has_down)(lambda: down_far(b, place(1, b, 0), 0).wait_send())
+    for k in (1, 2, 3):
+        out_z(k).wait_send()
+        out_x(k).wait_send()
+        out_y(k).wait_send()
+    out_core().wait()
     for p in range(3):
         for k in (1, 2, 3):
             ctx_copy(p, k).wait()
-    out[...] = gathered[...]
-
-
-def exchange_and_attend(frames, gain, w_query, w_key, w_value, band, lengths):
+    total = jnp.dot(gathered[:, :WIDTH], projection[0], preferred_element_type=jnp.float32)
+    for g in range(1, 4):
+        total += jnp.dot(
+            gathered[:, g * WIDTH:(g + 1) * WIDTH], projection[g], preferred_element_type=jnp.float32
+        )
+    out[...] = total.astype(jnp.bfloat16)
+
+
+def exchange_and_attend(frames, gain, w_query, w_key, w_value, band, lengths, w_out):
     vmem, smem, anywhere = (pl.BlockSpec(memory_space=m) for m in (pltpu.VMEM, pltpu.SMEM, pl.ANY))
     dma = pltpu.SemaphoreType.DMA
     bf16, f32 = jnp.bfloat16, jnp.float32
     return pl.pallas_call(
         kernel,
         out_shape=jax.ShapeDtypeStruct((ROWS, D), bf16),
-        in_specs=[vmem, vmem, anywhere, anywhere, anywhere, smem, smem],
+        in_specs=[vmem, vmem, anywhere, anywhere, anywhere, anywhere, smem, smem],
         out_specs=vmem,
         scratch_shapes=[
             pltpu.VMEM((D, 3 * WIDTH), bf16),
@@ -369,32 +432,28 @@
             pltpu.VMEM((ROWS, D), bf16),
             pltpu.VMEM((4, PIECE, 2 * WIDTH), bf16),
             pltpu.VMEM((4, PIECE, 2 * WIDTH), bf16),
+            pltpu.VMEM((4, WIDTH, D), bf16),
             dma((3,)), dma((3,)), dma((3,)),
             dma((4,)), dma((4,)), dma((4,)),
             dma((4,)), dma((4,)), dma((4,)), dma((4,)),
             dma((4, 4)), dma((4,)), dma((4, 4)), dma((4,)),
             dma((4,)), dma((4, 4)), dma((4,)), dma((4, 4)),
             dma((3, 3)), dma((3, 3)),
+            dma, dma((3,)), dma((3,)), dma((3,)), dma((3,)), dma((3,)), dma((3,)), dma, dma,
         ],
         compiler_params=pltpu.CompilerParams(
-            collective_id=0, has_side_effects=True, vmem_limit_bytes=48 * 2**20
+            collective_id=0, has_side_effects=True, vmem_limit_bytes=63 * 2**20
         ),
         cost_estimate=pl.CostEstimate(flops=60_000_000_000, bytes_accessed=8_000_000, transcendentals=8_000_000),
         name="attend",
-    )(frames, gain, w_query, w_key, w_value, band, lengths)
+    )(frames, gain, w_query, w_key, w_value, w_out, band, lengths)
 
 
 def local(frames, norm_gain, w_query, w_key, w_value, w_out, group_band, lengths):
-    frame_context = exchange_and_attend(
-        frames[0], norm_gain[None], w_query, w_key, w_value, group_band[0], lengths
+    update = exchange_and_attend(
+        frames[0], norm_gain[None], w_query, w_key, w_value, group_band[0], lengths, w_out
     )
-    full_rows = lax.all_gather(w_out, "head", axis=0, tiled=True)
-    update = jnp.dot(
-        frame_context,
-        lax.all_gather(full_rows, "dp", axis=1, tiled=True),
-        preferred_element_type=jnp.float32,
-    )
-    return update.astype(jnp.bfloat16)[None]
+    return update[None]
 
 
 def solution(mesh):

time: 198 us -> 122 us (0.62)
  the two profiles are of different devices: /device:TPU:396 before, /device:TPU:60 now
where the time goes in v2:
time: 122 us; the launch traced here: 121 us
  Pallas kernels  117 us (96%)
  local copies, waits for them, and re-layouts  3.1 us (3%)
    pallas_call x1, Pallas kernels, exchange_and_attend(): pl.pallas_call(kernel, out_shape=jax.ShapeDtypeStruct((ROWS, D), bf16), i...  117 us
    unnamed x6, local copies, waits for them, and re-layouts  2.5 us

profile of v2, /device:TPU:60, one launch (start us, length us, event | category | flops | bytes accessed | tf_op | source)
XLA Modules:
  0.0 121.3 jit_solution(11878785078970179566)
XLA Ops:
  0.0 0.0 copy-start.1
  0.0 0.0 copy-start
  0.7 0.0 copy-done.1
  0.7 0.6 copy.11
  1.3 0.0 copy-done
  1.3 0.6 broadcast_in_dim.6.gain
  1.9 117.5 %attend.1 = bf16[192,1536]{1,0:T(8,128)(2,1)} custom-call(bf16[192,1536]{1,0:T(8,128)(2,1)} %bitcast.7, f32[1,1536]{1,0:T(1,128)} %broadcast_in_dim.6.gain, bf16[768,384]{1,0:T(8,128)(2,1)} %w_query.1, bf16[768,384]{1,0:T(8,128)(2,1)} %w_key.1, bf16[768,384]{1,0:T(8,128)(2,1)} %w_value.1, bf16[384,768]{1,0:T(8,128)(2,1)} %w_out.1, s32[6,12]{1,0:T(8,128)} %bitcast.6, ...), custom_call_target="tpu_custom_call" | custom-call | flops 60000002048 | bytes 8000000 | tf_op jit(solution)/shard_map/attend/pallas_call | solution.py:417
  119.4 1.9 %copy.14 = bf16[1,192,1536]{2,1,0:T(8,128)(2,1)} copy(bf16[1,192,1536]{2,1,0:T(8,128)(2,1)} %bitcast.5) | data formatting | bytes 1179648
Async XLA Ops:
  0.0 0.7 copy-start.1
  0.0 1.3 %copy-start = (f32[1536]{0:T(1024)S(1)}, f32[1536]{0:T(1024)}, u32[]{:S(2)}) copy-start(f32[1536]{0:T(1024)} %param.9) | copy-start | bytes 18436

commit v3 on v2

--- a/solution.py
+++ b/solution.py
@@ -22,18 +22,26 @@
 
 
 def kernel(
-    frames, gain, w_query, w_key, w_value, w_out, band, lengths, out,
-    weights, normalized, query, kv, bias, onehot, acc, top, context, gathered, relay_up, relay_down, projection,
-    w_send, w_recv, w_local, left_send, right_send, block_recv,
+    frames, gain, w_query, w_key, w_value, w_out, marks, out,
+    weights, normalized, other_marks, query, kv, bias, onehot, acc, top, context, gathered, relay_up, relay_down, landed_up, landed_down, projection,
+    marks_send, marks_recv, w_send, w_recv, w_local, far_w_send, far_w_recv, line_w_send, line_w_recv, plane_w_send, plane_w_recv,
+    on_send, out_send, block_recv, core_send, core_recv,
     up_send, up_recv, down_send, down_recv,
     spread_up_send, spread_up_recv, spread_down_send, spread_down_recv,
     far_up_send, far_up_recv, far_down_send, far_down_recv,
+    last_up_send, last_up_recv, last_down_send, last_down_recv,
     ctx_send, ctx_recv,
     out_local, out_z_send, out_z_recv, out_x_send, out_x_recv, out_y_send, out_y_recv, out_core_send, out_core_recv,
 ):
     dp, seq, head = lax.axis_index("dp"), lax.axis_index("seq"), lax.axis_index("head")
     row, x = seq // 4, seq % 4
     y = seq // 16
+    utterance = head // 2
+    near = 1 - (dp + utterance) % 2
+    is_near = near == 1
+    group_of_heads = (head + 2 * (1 - near)) % 4
+    other_core = (1 - dp, seq, head)
+    place_on_line = head + dp * (3 - 2 * head)
     first_seq = row * 4
     has_up, has_down = row < 15, row > 0
 
@@ -47,36 +55,77 @@
     def greet(to):
         pl.semaphore_signal(barrier, inc=1, device_id=to, device_id_type=MESH)
 
-    greet((1 - dp, seq, head))
+    greet(other_core)
     for k in (1, 2, 3):
         greet((dp, seq, (head + k) % 4))
+        greet((1 - dp, seq, (head + k) % 4))
         greet((dp, first_seq + (x + k) % 4, head))
         greet((dp, (seq + 16 * k) % 64, head))
 
-    @pl.when((x == 0) & has_down)
-    def _():
-        for q in range(4):
-            greet((dp, first_seq - 4 + q, head))
-
-    @pl.when((x == 3) & has_up)
-    def _():
-        for q in range(4):
-            greet((dp, first_seq + 4 + q, head))
-
-    pl.semaphore_wait(barrier, 10 + (1 - (row + 1) // 16) + (row + 15) // 16)
+    pl.when(has_up)(lambda: greet((dp, (seq + 4) % 64, head)))
+    pl.when(has_down)(lambda: greet((dp, (seq + 60) % 64, head)))
+    pl.semaphore_wait(barrier, 13 + (1 - (row + 1) // 16) + (row + 15) // 16)
+
+    def swap_marks():
+        return copy(marks, other_marks, marks_send, marks_recv, other_core)
+
+    swap_marks().start()
 
     half = pl.ds(pl.multiple_of(dp * (D // 2), D // 2), D // 2)
 
     def weight_there(i, ref):
         part = weights.at[half, pl.ds(i * WIDTH, WIDTH)]
-        return copy(ref, part, w_send.at[i], w_recv.at[i], (1 - dp, seq, head))
+        return copy(ref, part, w_send.at[i], w_recv.at[i], other_core)
 
     def weight_here(i, ref):
         return pltpu.make_async_copy(ref, weights.at[half, pl.ds(i * WIDTH, WIDTH)], w_local.at[i])
 
+    first, second = (1 - dp) * y + dp * x, (1 - dp) * x + dp * y
+
+    def weight_far(i, ref):
+        start = first * ROWS + second * PIECE
+        return copy(
+            ref.at[pl.ds(pl.multiple_of(start, 16), PIECE), :],
+            weights.at[pl.ds(pl.multiple_of(dp * (D // 2) + start, 16), PIECE), pl.ds(i * WIDTH, WIDTH)],
+            far_w_send.at[i], far_w_recv.at[dp, i], (utterance, seq, (head + 2) % 4),
+        )
+
+    def weight_arrived(core, i, ref):
+        return copy(
+            ref.at[pl.ds(0, PIECE), :], weights.at[pl.ds(0, PIECE), pl.ds(i * WIDTH, WIDTH)],
+            far_w_send.at[i], far_w_recv.at[core, i], other_core,
+        )
+
+    def over_x(k):
+        return (dp, first_seq + (x + k) % 4, head)
+
+    def over_y(k):
+        return (dp, (seq + 16 * k) % 64, head)
+
+    def weight_line(core, k):
+        start = core * (D // 2) + (x * ROWS + y * PIECE if core else y * ROWS + x * PIECE)
+        part = weights.at[pl.ds(pl.multiple_of(start, 16), PIECE), :]
+        return copy(
+            part, part, line_w_send.at[core, k - 1], line_w_recv.at[core, k - 1], over_y(k) if core else over_x(k)
+        )
+
+    def weight_plane(core, k):
+        start = core * (D // 2) + (x if core else y) * ROWS
+        part = weights.at[pl.ds(pl.multiple_of(start, 16), ROWS), :]
+        return copy(
+            part, part, plane_w_send.at[core, k - 1], plane_w_recv.at[core, k - 1], over_x(k) if core else over_y(k)
+        )
+
     for i, ref in enumerate((w_query, w_key, w_value)):
-        weight_there(i, ref).start()
-        weight_here(i, ref).start()
+        weight_far(i, ref).start()
+
+        @pl.when(is_near)
+        def _():
+            weight_here(i, ref).start()
+
+        @pl.when(jnp.logical_not(is_near))
+        def _():
+            weight_there(i, ref).start()
 
     piece_rows = pl.ds(pl.multiple_of(y * 96 + x % 2 * 48, 16), 48)
     strip_rows = pl.ds(pl.multiple_of(y * 96, 16), 96)
@@ -113,25 +162,31 @@
     values = frames[...].astype(jnp.float32)
     center = values - jnp.mean(values, axis=-1, keepdims=True)
     spread = jnp.mean(center * center, axis=-1, keepdims=True)
-    normalized[head] = (center * lax.rsqrt(spread + epsilon) * gain[...]).astype(jnp.bfloat16)
-
-    has_left, has_right = head > 0, head < 3
-    left = (dp, seq, (head + 3) % 4)
-    right = (dp, seq, (head + 1) % 4)
-
-    def to_left(b):
-        return copy(normalized.at[b], normalized.at[b], left_send.at[b], block_recv.at[b], left)
-
-    def to_right(b):
-        return copy(normalized.at[b], normalized.at[b], right_send.at[b], block_recv.at[b], right)
-
-    pl.when(has_left)(lambda: to_left(head).start())
-    pl.when(has_right)(lambda: to_right(head).start())
+    normalized[head] = (center * lax.rsqrt(spread + epsilon) * gain[...][None, :]).astype(jnp.bfloat16)
+
+    step = 1 - 2 * dp
+    onward = (dp, seq, (head + 4 - step) % 4)
+    back = (dp, seq, (head + 4 + step) % 4)
+
+    def to_onward(b):
+        return copy(normalized.at[b], normalized.at[b], on_send.at[b], block_recv.at[b], onward)
+
+    def to_back():
+        return copy(normalized.at[head], normalized.at[head], out_send, block_recv.at[head], back)
+
+    def to_core(b):
+        return copy(normalized.at[b], normalized.at[4 + b], core_send.at[b], core_recv.at[b], other_core)
+
+    pl.when(place_on_line > 0)(lambda: to_onward(head).start())
+    pl.when(place_on_line == 0)(lambda: to_back().start())
 
     onehot[...] = (
         lax.broadcasted_iota(jnp.int32, (RUN, 128), 0) // GROUP
         == lax.broadcasted_iota(jnp.int32, (RUN, 128), 1)
     ).astype(jnp.bfloat16)
+    swap_marks().wait_recv()
+    seen_marks = marks[...] * near + other_marks[...] * (1 - near)
+    length = seen_marks[12:13, :]
     lane = lax.broadcasted_iota(jnp.int32, (1, 128), 1)
     within = lax.broadcasted_iota(jnp.int32, (GROUP, 128), 0)
     for kg in range(3 * REACH):
@@ -143,10 +198,10 @@
                 own = jnp.where(lane == g, 1, own)
             elif abs(offset) <= REACH:
                 column = offset + REACH if offset < 0 else offset + REACH - 1
-                seen = jnp.where(lane == g, band[g, column], seen)
+                seen = jnp.where(lane == g, seen_marks[column:column + 1, :], seen)
         group = seq * REACH - REACH + kg
         inside = jnp.where((group >= 0) & (group < 64 * REACH), 1, 0)
-        alive = (group * GROUP + within < lengths[0]).astype(jnp.int32) * inside
+        alive = (group * GROUP + within < length).astype(jnp.int32) * inside
         allowed = (jnp.where(seen == 1, 1, 0) * alive + own) > 0
         bias[kg * GROUP:(kg + 1) * GROUP, :] = jnp.where(allowed, 0.0, FORBIDDEN).astype(jnp.bfloat16)
 
@@ -158,9 +213,46 @@
     def _():
         kv[2 * RUN:3 * RUN, :] = jnp.zeros((RUN, 2 * WIDTH), jnp.bfloat16)
 
-    for i, ref in enumerate((w_query, w_key, w_value)):
-        weight_here(i, ref).wait()
-        weight_there(i, ref).wait_recv()
+    def spread_out_weights():
+        out_here().wait()
+        for k in (1, 2, 3):
+            out_z(k).wait_recv()
+        for k in (2, 1, 3):
+            out_x(k).start()
+
+    @pl.when(is_near)
+    def _():
+        for i, ref in enumerate((w_query, w_key, w_value)):
+            weight_here(i, ref).wait()
+            weight_there(i, ref).wait_recv()
+        spread_out_weights()
+
+    @pl.when(jnp.logical_not(is_near))
+    def _():
+        for core in range(2):
+            for i, ref in enumerate((w_query, w_key, w_value)):
+                weight_arrived(core, i, ref).wait_recv()
+            for k in (2, 1, 3):
+                weight_line(core, k).start()
+        spread_out_weights()
+        for core in range(2):
+            for k in (1, 2, 3):
+                weight_line(core, k).wait_recv()
+            for k in (2, 1, 3):
+                weight_plane(core, k).start()
+
+        @pl.when(place_on_line == 2)
+        def _():
+            to_onward(3 * utterance).wait_recv()
+            to_onward(3 * utterance).start()
+
+        for k in (1, 2, 3):
+            out_x(k).wait_recv()
+        for k in (2, 1, 3):
+            out_y(k).start()
+        for core in range(2):
+            for k in (1, 2, 3):
+                weight_plane(core, k).wait_recv()
 
     def place(side, b, q=None):
         start, size = side * RUN + b * ROWS, ROWS
@@ -185,41 +277,63 @@
             (dp, first_seq + q, head),
         )
 
-    def up_far(b, src, q):
-        return copy(src, place(0, b, q), far_up_send.at[b], far_up_recv.at[b, q], (dp, (first_seq + 4) % 64, head))
-
-    def down_far(b, src, q):
-        return copy(src, place(2, b, q), far_down_send.at[b], far_down_recv.at[b, q], (dp, (first_seq + 63) % 64, head))
-
-    sends_up_far, sends_down_far = (x == 3) & has_up, (x == 0) & has_down
-    relays_up, relays_down = (x < 3) & has_up, (x > 0) & has_down
-
-    def send_block(b):
+    def up_far(b, src, dst):
+        return copy(src, dst, far_up_send.at[b], far_up_recv.at[b], (dp, (seq + 4) % 64, head))
+
+    def down_far(b, src, dst):
+        return copy(src, dst, far_down_send.at[b], far_down_recv.at[b], (dp, (seq + 60) % 64, head))
+
+    def up_last(b, q):
+        return copy(
+            landed_up.at[b], place(0, b, q), last_up_send.at[b], last_up_recv.at[b, q], (dp, first_seq, head)
+        )
+
+    def down_last(b, q):
+        return copy(
+            landed_down.at[b], place(2, b, q), last_down_send.at[b], last_down_recv.at[b, q],
+            (dp, first_seq + 3, head),
+        )
+
+    def send_near(b):
         pl.when(x < 3)(lambda: up_near(b).start())
         pl.when(x > 0)(lambda: down_near(b).start())
 
-        @pl.when(sends_up_far)
+    def send_block(b):
+        @pl.when((x == 3) & has_up)
         def _():
             for q in range(3):
                 up_spread(b, q).start()
-            up_far(b, place(1, b, 3), 3).start()
-
-        @pl.when(sends_down_far)
+
+        @pl.when((x == 0) & has_down)
         def _():
             for q in range(1, 4):
                 down_spread(b, q).start()
-            down_far(b, place(1, b, 0), 0).start()
 
     def relay_block(b):
-        @pl.when(relays_up)
-        def _():
-            up_spread(b, x).wait_recv()
-            up_far(b, relay_up.at[b], x).start()
-
-        @pl.when(relays_down)
-        def _():
-            down_spread(b, x).wait_recv()
-            down_far(b, relay_down.at[b], x).start()
+        @pl.when(has_up)
+        def _():
+            pl.when(x < 3)(lambda: up_spread(b, x).wait_recv())
+            pl.when(x == 0)(lambda: up_far(b, relay_up.at[b], place(0, b, 0)).start())
+            pl.when((x > 0) & (x < 3))(lambda: up_far(b, relay_up.at[b], landed_up.at[b]).start())
+            pl.when(x == 3)(lambda: up_far(b, place(1, b, 3), landed_up.at[b]).start())
+
+        @pl.when(has_down)
+        def _():
+            pl.when(x > 0)(lambda: down_spread(b, x).wait_recv())
+            pl.when(x == 3)(lambda: down_far(b, relay_down.at[b], place(2, b, 3)).start())
+            pl.when((x > 0) & (x < 3))(lambda: down_far(b, relay_down.at[b], landed_down.at[b]).start())
+            pl.when(x == 0)(lambda: down_far(b, place(1, b, 0), landed_down.at[b]).start())
+
+    def deliver_block(b):
+        @pl.when((x > 0) & has_down)
+        def _():
+            up_far(b, relay_up.at[b], landed_up.at[b]).wait_recv()
+            up_last(b, x).start()
+
+        @pl.when((x < 3) & has_up)
+        def _():
+            down_far(b, relay_down.at[b], landed_down.at[b]).wait_recv()
+            down_last(b, x).start()
 
     far_end = head // 2
     mirrored = head + far_end * (3 - 2 * head)
@@ -231,37 +345,44 @@
     def project(t, carry):
         b = nth(t)
 
-        @pl.when(t > 0)
-        def _():
-            to_left(b).wait_recv()
-            pl.when((b < head) & has_right)(lambda: to_right(b).start())
-            pl.when((b > head) & has_left)(lambda: to_left(b).start())
-
-        @pl.when(t == 1)
-        def _():
-            out_here().wait()
-            for k in (1, 2, 3):
-                out_z(k).wait_recv()
-            for k in (2, 1, 3):
-                out_x(k).start()
-
-        @pl.when(t == 2 + mirrored)
+        @pl.when(is_near)
+        def _():
+            pl.when(t > 0)(lambda: to_onward(b).wait_recv())
+            pl.when((place_on_line == 1) & (t > 1))(lambda: to_onward(b).start())
+            to_core(b).start()
+
+        @pl.when(jnp.logical_not(is_near))
+        def _():
+            to_core(b).wait_recv()
+
+        @pl.when(is_near & (t == 2))
         def _():
             for k in (1, 2, 3):
                 out_x(k).wait_recv()
             for k in (2, 1, 3):
                 out_y(k).start()
 
-        rows = normalized[b]
+        rows = normalized[b + 4 * (1 - near)]
         product = jnp.dot(rows, weights[...], preferred_element_type=jnp.float32).astype(jnp.bfloat16)
         start = pl.multiple_of(b * ROWS, ROWS)
         query[pl.ds(start, ROWS), :] = product[:, :WIDTH] * jnp.bfloat16(0.125)
         kv[pl.ds(pl.multiple_of(RUN + start, ROWS), ROWS), :] = product[:, WIDTH:]
         send_block(b)
-        pl.when(t > 0)(lambda: relay_block(nth((t + 3) % 4)))
+        pl.when(is_near)(lambda: send_near(b))
         return carry
 
     lax.fori_loop(0, 4, project, 0)
+
+    def relay(t, carry):
+        relay_block(nth(t))
+        return carry
+
+    lax.fori_loop(0, 4, relay, 0)
+
+    @pl.when(jnp.logical_not(is_near))
+    def _():
+        for t in range(4):
+            send_near(nth(t))
 
     low_half = lax.broadcasted_iota(jnp.int32, (QB, 128), 1) < HD
 
@@ -297,7 +418,13 @@
     def own_part(p, carry):
         for j in range(3):
             attend(p, j * QB, RUN, RUN, True)
-        pl.when(p == 0)(lambda: relay_block(nth(3)))
+
+        @pl.when(p == 0)
+        def _():
+            deliver_block(nth(0))
+            deliver_block(nth(1))
+
+        pl.when(p > 0)(lambda: deliver_block(nth(p + 1)))
         return carry
 
     lax.fori_loop(0, 3, own_part, 0)
@@ -313,8 +440,9 @@
             @pl.when((x == 0) & has_down)
             def _():
                 for b in range(4):
-                    for q in range(4):
-                        up_far(b, place(1, b, q), q).wait_recv()
+                    up_far(b, relay_up.at[b], place(0, b, 0)).wait_recv()
+                    for q in range(1, 4):
+                        up_last(b, q).wait_recv()
 
         @pl.when(side == 1)
         def _():
@@ -326,8 +454,9 @@
             @pl.when((x == 3) & has_up)
             def _():
                 for b in range(4):
-                    for q in range(4):
-                        down_far(b, place(1, b, q), q).wait_recv()
+                    down_far(b, relay_down.at[b], place(2, b, 3)).wait_recv()
+                    for q in range(3):
+                        down_last(b, q).wait_recv()
 
     def side_part(p, side):
         for j in range(3):
@@ -349,13 +478,15 @@
     last_side = 1 - first_side
     wait_side(last_side)
 
-    def ctx_copy(p, k):
-        to = (head + k) % 4
-        return copy(
-            context.at[pl.ds(pl.multiple_of(to * ROWS, ROWS), ROWS), pl.ds(pl.multiple_of(p * 128, 128), 128)],
-            gathered.at[:, pl.ds(pl.multiple_of(head * WIDTH + p * 128, 128), 128)],
-            ctx_send.at[p, k - 1], ctx_recv.at[p, k - 1], (dp, seq, to),
-        )
+    def ctx_copy(p, to, heads):
+        return copy(
+            context.at[pl.ds(to * ROWS, ROWS), pl.ds(pl.multiple_of(p * 128, 128), 128)],
+            gathered.at[:, pl.ds(pl.multiple_of(heads * WIDTH + p * 128, 128), 128)],
+            ctx_send.at[p, to], ctx_recv.at[p, heads], (utterance, seq, to),
+        )
+
+    def keeps(to):
+        return is_near & (head == to)
 
     def late_part(p, carry):
         side_part(p, last_side)
@@ -366,42 +497,67 @@
             context[rows, lanes] = jnp.where(
                 low_half, low[:, :128] / low[:, 128:], high[:, :128] / high[:, 128:]
             ).astype(jnp.bfloat16)
-        for k in (2, 1, 3):
-            ctx_copy(p, k).start()
+        for to in range(4):
+            pl.when(jnp.logical_not(keeps(to)))(lambda: ctx_copy(p, to, group_of_heads).start())
         return carry
 
     lax.fori_loop(0, 3, late_part, 0)
-    own_lanes = pl.ds(pl.multiple_of(head * WIDTH, 128), WIDTH)
-    gathered[:, own_lanes] = context[pl.ds(pl.multiple_of(head * ROWS, ROWS), ROWS), :]
-
+
+    @pl.when(is_near)
+    def _():
+        own_lanes = pl.ds(pl.multiple_of(head * WIDTH, 128), WIDTH)
+        gathered[:, own_lanes] = context[pl.ds(pl.multiple_of(head * ROWS, ROWS), ROWS), :]
+
+    swap_marks().wait_send()
     for i, ref in enumerate((w_query, w_key, w_value)):
-        weight_there(i, ref).wait_send()
+        weight_far(i, ref).wait_send()
+
+    @pl.when(jnp.logical_not(is_near))
+    def _():
+        for i, ref in enumerate((w_query, w_key, w_value)):
+            weight_there(i, ref).wait_send()
+        for core in range(2):
+            for k in (1, 2, 3):
+                weight_line(core, k).wait_send()
+                weight_plane(core, k).wait_send()
+
+    pl.when(place_on_line > 0)(lambda: to_onward(head).wait_send())
+    pl.when(place_on_line == 0)(lambda: to_back().wait_send())
+    pl.when(place_on_line == 2)(lambda: to_onward(3 * utterance).wait_send())
+
+    @pl.when(place_on_line == 1)
+    def _():
+        for t in (2, 3):
+            to_onward(nth(t)).wait_send()
+
     for b in range(4):
-        pl.when((b <= head) & has_right)(lambda: to_right(b).wait_send())
-        pl.when((b >= head) & has_left)(lambda: to_left(b).wait_send())
+        pl.when(is_near)(lambda: to_core(b).wait_send())
         pl.when(x < 3)(lambda: up_near(b).wait_send())
         pl.when(x > 0)(lambda: down_near(b).wait_send())
 
-        @pl.when(sends_up_far)
+        @pl.when((x == 3) & has_up)
         def _():
             for q in range(3):
                 up_spread(b, q).wait_send()
 
-        @pl.when(sends_down_far)
+        @pl.when((x == 0) & has_down)
         def _():
             for q in range(1, 4):
                 down_spread(b, q).wait_send()
 
-        pl.when(has_up)(lambda: up_far(b, place(1, b, 3), 3).wait_send())
-        pl.when(has_down)(lambda: down_far(b, place(1, b, 0), 0).wait_send())
+        pl.when(has_up)(lambda: up_far(b, relay_up.at[b], landed_up.at[b]).wait_send())
+        pl.when(has_down)(lambda: down_far(b, relay_down.at[b], landed_down.at[b]).wait_send())
+        pl.when((x > 0) & has_down)(lambda: up_last(b, x).wait_send())
+        pl.when((x < 3) & has_up)(lambda: down_last(b, x).wait_send())
     for k in (1, 2, 3):
         out_z(k).wait_send()
         out_x(k).wait_send()
         out_y(k).wait_send()
     out_core().wait()
-    for p in range(3):
-        for k in (1, 2, 3):
-            ctx_copy(p, k).wait()
+    for g in range(4):
+        for p in range(3):
+            pl.when(jnp.logical_not(keeps(g)))(lambda: ctx_copy(p, g, group_of_heads).wait_send())
+            pl.when(jnp.logical_not(keeps(g)))(lambda: ctx_copy(p, g, g).wait_recv())
     total = jnp.dot(gathered[:, :WIDTH], projection[0], preferred_element_type=jnp.float32)
     for g in range(1, 4):
         total += jnp.dot(
@@ -410,18 +566,19 @@
     out[...] = total.astype(jnp.bfloat16)
 
 
-def exchange_and_attend(frames, gain, w_query, w_key, w_value, band, lengths, w_out):
-    vmem, smem, anywhere = (pl.BlockSpec(memory_space=m) for m in (pltpu.VMEM, pltpu.SMEM, pl.ANY))
+def exchange_and_attend(frames, gain, w_query, w_key, w_value, w_out, marks):
+    vmem, anywhere = (pl.BlockSpec(memory_space=m) for m in (pltpu.VMEM, pl.ANY))
     dma = pltpu.SemaphoreType.DMA
     bf16, f32 = jnp.bfloat16, jnp.float32
     return pl.pallas_call(
         kernel,
         out_shape=jax.ShapeDtypeStruct((ROWS, D), bf16),
-        in_specs=[vmem, vmem, anywhere, anywhere, anywhere, anywhere, smem, smem],
+        in_specs=[vmem, vmem, anywhere, anywhere, anywhere, anywhere, vmem],
         out_specs=vmem,
         scratch_shapes=[
             pltpu.VMEM((D, 3 * WIDTH), bf16),
-            pltpu.VMEM((4, ROWS, D), bf16),
+            pltpu.VMEM((8, ROWS, D), bf16),
+            pltpu.VMEM((16, 128), jnp.int32),
             pltpu.VMEM((RUN, WIDTH), bf16),
             pltpu.VMEM((3 * RUN, 2 * WIDTH), bf16),
             pltpu.VMEM((3 * RUN, 128), bf16),
@@ -432,13 +589,17 @@
             pltpu.VMEM((ROWS, D), bf16),
             pltpu.VMEM((4, PIECE, 2 * WIDTH), bf16),
             pltpu.VMEM((4, PIECE, 2 * WIDTH), bf16),
+            pltpu.VMEM((4, PIECE, 2 * WIDTH), bf16),
+            pltpu.VMEM((4, PIECE, 2 * WIDTH), bf16),
             pltpu.VMEM((4, WIDTH, D), bf16),
-            dma((3,)), dma((3,)), dma((3,)),
-            dma((4,)), dma((4,)), dma((4,)),
+            dma, dma, dma((3,)), dma((3,)), dma((3,)),
+            dma((3,)), dma((2, 3)), dma((2, 3)), dma((2, 3)), dma((2, 3)), dma((2, 3)),
+            dma((4,)), dma, dma((4,)), dma((4,)), dma((4,)),
             dma((4,)), dma((4,)), dma((4,)), dma((4,)),
             dma((4, 4)), dma((4,)), dma((4, 4)), dma((4,)),
+            dma((4,)), dma((4,)), dma((4,)), dma((4,)),
             dma((4,)), dma((4, 4)), dma((4,)), dma((4, 4)),
-            dma((3, 3)), dma((3, 3)),
+            dma((3, 4)), dma((3, 4)),
             dma, dma((3,)), dma((3,)), dma((3,)), dma((3,)), dma((3,)), dma((3,)), dma, dma,
         ],
         compiler_params=pltpu.CompilerParams(
@@ -446,13 +607,13 @@
         ),
         cost_estimate=pl.CostEstimate(flops=60_000_000_000, bytes_accessed=8_000_000, transcendentals=8_000_000),
         name="attend",
-    )(frames, gain, w_query, w_key, w_value, w_out, band, lengths)
+    )(frames, gain, w_query, w_key, w_value, w_out, marks)
 
 
 def local(frames, norm_gain, w_query, w_key, w_value, w_out, group_band, lengths):
-    update = exchange_and_attend(
-        frames[0], norm_gain[None], w_query, w_key, w_value, group_band[0], lengths, w_out
-    )
+    band = jnp.pad(group_band[0].T, ((0, 4), (0, 128 - REACH)))
+    marks = jnp.where(lax.broadcasted_iota(jnp.int32, (16, 128), 0) == 12, lengths[0], band)
+    update = exchange_and_attend(frames[0], norm_gain, w_query, w_key, w_value, w_out, marks)
     return update[None]
 
 

time: 122 us -> 111 us (0.910)
  the two profiles are of different devices: /device:TPU:60 before, /device:TPU:25 now
where the time goes in v3:
time: 111 us
  Pallas kernels  107 us (96%)
  local copies, waits for them, and re-layouts  2.68 us (2%)
    pallas_call x1, Pallas kernels, exchange_and_attend(): pl.pallas_call(kernel, out_shape=jax.ShapeDtypeStruct((ROWS, D), bf16), i...  107 us
    unnamed x3, local copies, waits for them, and re-layouts  2.58 us

profile of v3, /device:TPU:25, one launch (start us, length us, event | category | flops | bytes accessed | tf_op | source)
XLA Modules:
  0.0 110.6 jit_solution(12649633912887018620)
XLA Ops:
  0.7 0.0 copy-start
  0.7 0.7 copy-done
  1.3 0.1 copy.10
  1.4 0.7 pad_select_fusion.marks
  2.1 106.6 %attend.1 = bf16[192,1536]{1,0:T(8,128)(2,1)} custom-call(bf16[192,1536]{1,0:T(8,128)(2,1)} %bitcast.9, f32[1536]{0:T(1024)} %gain.1, bf16[768,384]{1,0:T(8,128)(2,1)} %w_query.1, bf16[768,384]{1,0:T(8,128)(2,1)} %w_key.1, bf16[768,384]{1,0:T(8,128)(2,1)} %w_value.1, bf16[384,768]{1,0:T(8,128)(2,1)} %w_out.1, s32[16,128]{1,0:T(8,128)} %pad_select_fusion.marks), custom_call_target="tpu_custom_call" | custom-call | flops 60000002048 | bytes 8000000 | tf_op jit(solution)/shard_map/attend/pallas_call | solution.py:573
  108.7 1.9 %copy.13 = bf16[1,192,1536]{2,1,0:T(8,128)(2,1)} copy(bf16[1,192,1536]{2,1,0:T(8,128)(2,1)} %bitcast.7) | data formatting | bytes 1179648
  (1 shorter events, 0.0 us)
Async XLA Ops:
  0.7 0.7 copy-start

commit v4 on v3

--- a/solution.py
+++ b/solution.py
@@ -355,7 +355,7 @@
         def _():
             to_core(b).wait_recv()
 
-        @pl.when(is_near & (t == 2))
+        @pl.when(is_near & (t == 1))
         def _():
             for k in (1, 2, 3):
                 out_x(k).wait_recv()
@@ -377,12 +377,12 @@
         relay_block(nth(t))
         return carry
 
-    lax.fori_loop(0, 4, relay, 0)
-
     @pl.when(jnp.logical_not(is_near))
     def _():
         for t in range(4):
             send_near(nth(t))
+
+    lax.fori_loop(0, 4, relay, 0)
 
     low_half = lax.broadcasted_iota(jnp.int32, (QB, 128), 1) < HD
 
@@ -465,6 +465,9 @@
             attend(p, query_start, key_start, RUN - j * QB, False)
 
     first_side = 1 - (x + 3) // 4
+    for k in (1, 2, 3):
+        out_y(k).wait_recv()
+    out_core().start()
     wait_side(first_side)
 
     def early_part(p, carry):
@@ -472,9 +475,6 @@
         return carry
 
     lax.fori_loop(0, 3, early_part, 0)
-    for k in (1, 2, 3):
-        out_y(k).wait_recv()
-    out_core().start()
     last_side = 1 - first_side
     wait_side(last_side)
 
@@ -554,16 +554,17 @@
         out_x(k).wait_send()
         out_y(k).wait_send()
     out_core().wait()
+    total = jnp.zeros((ROWS, D), jnp.float32)
     for g in range(4):
         for p in range(3):
-            pl.when(jnp.logical_not(keeps(g)))(lambda: ctx_copy(p, g, group_of_heads).wait_send())
             pl.when(jnp.logical_not(keeps(g)))(lambda: ctx_copy(p, g, g).wait_recv())
-    total = jnp.dot(gathered[:, :WIDTH], projection[0], preferred_element_type=jnp.float32)
-    for g in range(1, 4):
         total += jnp.dot(
             gathered[:, g * WIDTH:(g + 1) * WIDTH], projection[g], preferred_element_type=jnp.float32
         )
     out[...] = total.astype(jnp.bfloat16)
+    for p in range(3):
+        for to in range(4):
+            pl.when(jnp.logical_not(keeps(to)))(lambda: ctx_copy(p, to, group_of_heads).wait_send())
 
 
 def exchange_and_attend(frames, gain, w_query, w_key, w_value, w_out, marks):

time: 111 us -> 107 us (0.964)
  Pallas kernels: 107 us -> 103 us
    pallas_call x1, Pallas kernels: 107 us -> 103 us  [exchange_and_attend(): pl.pallas_call(kernel, out_shape=jax.ShapeDtypeStruct((ROWS, D), bf16), i...]
where the time goes in v4:
time: 107 us
  Pallas kernels  103 us (96%)
  local copies, waits for them, and re-layouts  2.68 us (3%)
    pallas_call x1, Pallas kernels, exchange_and_attend(): pl.pallas_call(kernel, out_shape=jax.ShapeDtypeStruct((ROWS, D), bf16), i...  103 us
    unnamed x3, local copies, waits for them, and re-layouts  2.58 us

profile of v4, /device:TPU:25, one launch (start us, length us, event | category | flops | bytes accessed | tf_op | source)
XLA Modules:
  0.0 107.1 jit_solution(443591730161887930)
XLA Ops:
  0.7 0.0 copy-start
  0.7 0.7 copy-done
  1.3 0.1 copy.10
  1.4 0.7 pad_select_fusion.marks
  2.1 103.1 %attend.1 = bf16[192,1536]{1,0:T(8,128)(2,1)} custom-call(bf16[192,1536]{1,0:T(8,128)(2,1)} %bitcast.9, f32[1536]{0:T(1024)} %gain.1, bf16[768,384]{1,0:T(8,128)(2,1)} %w_query.1, bf16[768,384]{1,0:T(8,128)(2,1)} %w_key.1, bf16[768,384]{1,0:T(8,128)(2,1)} %w_value.1, bf16[384,768]{1,0:T(8,128)(2,1)} %w_out.1, s32[16,128]{1,0:T(8,128)} %pad_select_fusion.marks), custom_call_target="tpu_custom_call" | custom-call | flops 60000002048 | bytes 8000000 | tf_op jit(solution)/shard_map/attend/pallas_call | solution.py:574
  105.2 1.9 %copy.13 = bf16[1,192,1536]{2,1,0:T(8,128)(2,1)} copy(bf16[1,192,1536]{2,1,0:T(8,128)(2,1)} %bitcast.7) | data formatting | bytes 1179648
  (1 shorter events, 0.0 us)
Async XLA Ops:
  0.7 0.7 copy-start

commit v5 on v4

--- a/solution.py
+++ b/solution.py
@@ -480,7 +480,7 @@
 
     def ctx_copy(p, to, heads):
         return copy(
-            context.at[pl.ds(to * ROWS, ROWS), pl.ds(pl.multiple_of(p * 128, 128), 128)],
+            context.at[pl.ds(pl.multiple_of(to * ROWS, ROWS), ROWS), pl.ds(pl.multiple_of(p * 128, 128), 128)],
             gathered.at[:, pl.ds(pl.multiple_of(heads * WIDTH + p * 128, 128), 128)],
             ctx_send.at[p, to], ctx_recv.at[p, heads], (utterance, seq, to),
         )
@@ -497,7 +497,8 @@
             context[rows, lanes] = jnp.where(
                 low_half, low[:, :128] / low[:, 128:], high[:, :128] / high[:, 128:]
             ).astype(jnp.bfloat16)
-        for to in range(4):
+        for n in range(4):
+            to = 3 - n + utterance * (2 * n - 3)
             pl.when(jnp.logical_not(keeps(to)))(lambda: ctx_copy(p, to, group_of_heads).start())
         return carry
 

time: 107 us -> 107 us (level)
  no operation moved by 1% of the time
where the time goes in v5:
time: 107 us
  Pallas kernels  103 us (96%)
  local copies, waits for them, and re-layouts  2.68 us (3%)
    pallas_call x1, Pallas kernels, exchange_and_attend(): pl.pallas_call(kernel, out_shape=jax.ShapeDtypeStruct((ROWS, D), bf16), i...  103 us
    unnamed x3, local copies, waits for them, and re-layouts  2.58 us

profile of v5, /device:TPU:25, one launch (start us, length us, event | category | flops | bytes accessed | tf_op | source)
XLA Modules:
  0.0 107.2 jit_solution(11756605020764243565)
XLA Ops:
  0.7 0.0 copy-start
  0.7 0.7 copy-done
  1.3 0.1 copy.10
  1.4 0.7 pad_select_fusion.marks
  2.1 103.1 %attend.1 = bf16[192,1536]{1,0:T(8,128)(2,1)} custom-call(bf16[192,1536]{1,0:T(8,128)(2,1)} %bitcast.9, f32[1536]{0:T(1024)} %gain.1, bf16[768,384]{1,0:T(8,128)(2,1)} %w_query.1, bf16[768,384]{1,0:T(8,128)(2,1)} %w_key.1, bf16[768,384]{1,0:T(8,128)(2,1)} %w_value.1, bf16[384,768]{1,0:T(8,128)(2,1)} %w_out.1, s32[16,128]{1,0:T(8,128)} %pad_select_fusion.marks), custom_call_target="tpu_custom_call" | custom-call | flops 60000002048 | bytes 8000000 | tf_op jit(solution)/shard_map/attend/pallas_call | solution.py:575
  105.2 1.9 %copy.13 = bf16[1,192,1536]{2,1,0:T(8,128)(2,1)} copy(bf16[1,192,1536]{2,1,0:T(8,128)(2,1)} %bitcast.7) | data formatting | bytes 1179648
  (1 shorter events, 0.0 us)
Async XLA Ops:
  0.7 0.7 copy-start
